TPU v7x, 32 devices: a whole 2x2x4 slice. The times are simulated.
32 devices in a mesh: groups: 2 (over y), tm: 4 (over z), space: 2 (over x), clip: 2 (over core).
Axes of the slice: x: 2, y: 2, z: 4, core: 2. Of those that a mesh axis runs over, the one named last changes fastest.
Arguments:
- latents: bfloat16 [4, 16, 8, 6144], P(('groups', 'clip'), 'tm', 'space'), parts along dimension 0, may hold values from -6 to 6
- frame_counts: int32 [4], P(('groups', 'clip')), parts along dimension 0, may hold values from 2 to 16, as said below
- gain_first: float32 [192], replicated, may hold values from 0.5 to 1.5
- bias_first: float32 [192], replicated, may hold values from -3 to 3
- weight_first: bfloat16 [3, 3, 3, 192, 192], replicated, may hold values from -0.078125 to 0.078125
- gain_second: float32 [192], replicated, may hold values from 0.5 to 1.5
- bias_second: float32 [192], replicated, may hold values from -3 to 3
- weight_second: bfloat16 [3, 3, 3, 192, 192], replicated, may hold values from -0.078125 to 0.078125
Outputs:
- encoded: bfloat16 [4, 16, 8, 6144], P(('groups', 'clip'), 'tm', 'space'), parts along dimension 0
There are 2 independent parts, one for each index of `groups`. A program takes and returns all parts, laid end to end along the dimension named above; an argument that names none is the same for every part. Nothing has to cross between parts.
Inputs may be any that keep to these rules, and one draw needn't show every extreme that they name: `frame_counts`: in every part exactly one clip has all 16 frames valid; every other clip has fewer.
All inputs are finite; a program needn't handle non-finite values.
Results may differ from a plain program's by a relative error of at most 0.007.
Values may be sent and summed in bfloat16 or wider, within the bound.
A program may use at most 64 MiB of HBM per device.

v0:
```python
import jax
import jax.numpy as jnp
from jax import lax
from jax.sharding import PartitionSpec as P


def from_behind(x, axis, by):
    size = lax.axis_size(axis)
    pairs = [(i, i + by) for i in range(size) if 0 <= i + by < size]
    return lax.ppermute(x, axis, pairs)


def padded_2(x, sides, width):
    for axis, dim in sides:
        size, length = (lax.axis_size(axis), x.shape[dim])
        up = [(i, (i + 1) % size) for i in range(size - 1)]
        down = [(j, i) for i, j in up]
        last = lax.slice_in_dim(x, length - width, length, axis=dim)
        first = lax.slice_in_dim(x, 0, width, axis=dim)
        before = lax.ppermute(last, axis, up)
        after = lax.ppermute(first, axis, down)
        x = jnp.concatenate([before, x, after], axis=dim)
    return x


def norm_silu(values, gain):
    values = values.astype(jnp.float32)
    mean_square = jnp.mean(values * values, axis=-1, keepdims=True)
    scaled = values * lax.rsqrt(mean_square + 1e-06) * gain
    return jax.nn.silu(scaled).astype(jnp.bfloat16)


def conv_local(widened, kernel, out_frames, out_rows):
    channels = widened.shape[3]
    band_cols = widened.shape[2]
    padded = jnp.pad(widened, ((0, 0), (0, 0), (1, 1), (0, 0)))
    stacked = jnp.concatenate(
        [
            padded[:, :, 0:band_cols],
            padded[:, :, 1 : band_cols + 1],
            padded[:, :, 2 : band_cols + 2],
        ],
        axis=3,
    )
    merged = kernel.reshape(3, 3, 3 * channels, channels)
    total = jnp.zeros((out_frames * out_rows * band_cols, channels), jnp.float32)
    for shift_time in range(3):
        for shift_row in range(3):
            patch_rows = stacked[
                shift_time : shift_time + out_frames, shift_row : shift_row + out_rows
            ]
            total = total + jnp.dot(
                patch_rows.reshape(-1, 3 * channels),
                merged[shift_time, shift_row],
                preferred_element_type=jnp.float32,
            )
    return total.reshape(out_frames, out_rows, band_cols, channels)


def shards(
    latents,
    frame_counts,
    gain_first,
    bias_first,
    weight_first,
    gain_second,
    bias_second,
    weight_second,
):
    channels = gain_first.shape[0]
    span_frames, band_rows, flat_width = (latents.shape[1], latents.shape[2], latents.shape[3])
    band_cols = flat_width // channels
    limit_frames = frame_counts[0]
    first_frame = lax.axis_index("tm") * span_frames
    first_row = lax.axis_index("space") * band_rows
    total_rows = band_rows * lax.axis_size("space")
    frame_index = first_frame + jnp.arange(span_frames, dtype=jnp.int32)
    frame_mask = (frame_index < limit_frames)[:, None, None, None]
    shaped = latents[0].reshape(span_frames, band_rows, band_cols, channels)
    masked_input = jnp.where(frame_mask, shaped, jnp.zeros_like(shaped))
    flat_input = masked_input.reshape(span_frames, band_rows, flat_width)
    earlier = from_behind(flat_input, "tm", 1)
    joined = jnp.concatenate([earlier, flat_input], axis=0)
    rimmed = padded_2(joined, (("space", 1),), 2)
    window = rimmed.reshape(span_frames + 4, band_rows + 4, band_cols, channels)
    normed_first = norm_silu(window, gain_first)
    convolved = conv_local(normed_first, weight_first, span_frames + 2, band_rows + 2)
    wide_frames = first_frame - 2 + jnp.arange(span_frames + 2, dtype=jnp.int32)
    wide_rows = first_row - 1 + jnp.arange(band_rows + 2, dtype=jnp.int32)
    keep_frames = (wide_frames >= 0) & (wide_frames < limit_frames)
    keep_rows = (wide_rows >= 0) & (wide_rows < total_rows)
    keep_both = keep_frames[:, None, None, None] & keep_rows[None, :, None, None]
    hidden_first = jnp.where(keep_both, convolved + bias_first, 0.0).astype(jnp.bfloat16)
    widened_second = norm_silu(hidden_first, gain_second)
    second = conv_local(widened_second, weight_second, span_frames, band_rows)
    summed = masked_input.astype(jnp.float32) + second + bias_second
    encoded = jnp.where(frame_mask, summed, 0.0).astype(jnp.bfloat16)
    return encoded.reshape(1, span_frames, band_rows, flat_width)


def solution(mesh):
    return jax.shard_map(
        shards,
        mesh=mesh,
        in_specs=(
            P(("groups", "clip"), "tm", "space", None),
            P(("groups", "clip")),
            P(),
            P(),
            P(),
            P(),
            P(),
            P(),
        ),
        out_specs=P(("groups", "clip"), "tm", "space", None),
        check_vma=False,
    )
```

profile of v0, /device:TPU:8, one launch (start us, length us, event | category | flops | bytes accessed | tf_op | source)
XLA Modules:
  0.0 45.9 jit_solution(9589094844563484832)
XLA Ops:
  0.7 1.1 %bitcast_select_fusion = bf16[4,4,6144]{2,1,0:T(4,128)(2,1)S(1)} fusion(bf16[1,4,4,6144]{3,2,1,0:T(4,128)(2,1)} %param.8, pred[4]{0:T(512)(128)(4,1)S(1)} %add_compare_fusion), kind=kLoop, calls=%fused_computation.54 | loop fusion | flops 98304 | bytes 393220 | tf_op jit(solution)/shard_map/jit(_where)/select_n | solution.py:80
  1.8 3.5 %collective-permute-start = (bf16[4,4,6144]{2,1,0:T(4,128)(2,1)S(1)}, bf16[4,4,6144]{2,1,0:T(4,128)(2,1)S(1)}, u32[]{:S(2)}, u32[]{:S(2)}) collective-permute-start(bf16[4,4,6144]{2,1,0:T(4,128)(2,1)S(1)} %bitcast_select_fusion), channel_id=1, source_target_pairs={{0,4},{4,8},{8,12},{1,5},{5,9},{9,13},{2,6},{6,10},{10,14},{3,7},{... | collective-permute-start | bytes 589832 | tf_op jit(solution)/shard_map/ppermute | solution.py:10
  5.3 5.0 %collective-permute-done = bf16[4,4,6144]{2,1,0:T(4,128)(2,1)S(1)} collective-permute-done((bf16[4,4,6144]{2,1,0:T(4,128)(2,1)S(1)}, bf16[4,4,6144]{2,1,0:T(4,128)(2,1)S(1)}, u32[]{:S(2)}, u32[]{:S(2)}) %collective-permute-start) | collective-permute-done | bytes 196640 | tf_op jit(solution)/shard_map/ppermute | solution.py:10
  10.3 0.3 fusion.2
  10.6 3.4 %collective-permute-start.1 = (bf16[8,2,6144]{2,1,0:T(2,128)(2,1)S(1)}, bf16[8,2,6144]{2,1,0:T(2,128)(2,1)S(1)}, u32[]{:S(2)}, u32[]{:S(2)}) collective-permute-start(bf16[8,2,6144]{2,1,0:T(2,128)(2,1)S(1)} %get-tuple-element.27), channel_id=1, source_target_pairs={{0,2},{1,3},{4,6},{5,7},{8,10},{9,11},{12,14},{13,15},{16,18},{17,... | collective-permute-start | bytes 589832 | tf_op jit(solution)/shard_map/ppermute | solution.py:20
  14.0 1.3 %collective-permute-start.2 = (bf16[8,2,6144]{2,1,0:T(2,128)(2,1)S(1)}, bf16[8,2,6144]{2,1,0:T(2,128)(2,1)S(1)}, u32[]{:S(2)}, u32[]{:S(2)}) collective-permute-start(bf16[8,2,6144]{2,1,0:T(2,128)(2,1)S(1)} %get-tuple-element.28), channel_id=1, source_target_pairs={{2,0},{3,1},{6,4},{7,5},{10,8},{11,9},{14,12},{15,13},{18,16},{19,... | collective-permute-start | bytes 589832 | tf_op jit(solution)/shard_map/ppermute | solution.py:21
  15.4 0.1 broadcast_in_dim.60
  15.5 0.1 broadcast_in_dim.61
  15.6 0.7 %add.178 = f32[32,192]{1,0:T(8,128)S(1)} broadcast(f32[192]{0:T(256)} %param.14), dimensions={1} | broadcast | bytes 25344 | tf_op jit(solution)/shard_map/add | solution.py:96
  16.3 0.1 add.179
  16.3 0.9 %collective-permute-done.1 = bf16[8,2,6144]{2,1,0:T(2,128)(2,1)S(1)} collective-permute-done((bf16[8,2,6144]{2,1,0:T(2,128)(2,1)S(1)}, bf16[8,2,6144]{2,1,0:T(2,128)(2,1)S(1)}, u32[]{:S(2)}, u32[]{:S(2)}) %collective-permute-start.1) | collective-permute-done | bytes 196640 | tf_op jit(solution)/shard_map/ppermute | solution.py:20
  17.3 4.3 %collective-permute-done.2 = bf16[8,2,6144]{2,1,0:T(2,128)(2,1)S(1)} collective-permute-done((bf16[8,2,6144]{2,1,0:T(2,128)(2,1)S(1)}, bf16[8,2,6144]{2,1,0:T(2,128)(2,1)S(1)}, u32[]{:S(2)}, u32[]{:S(2)}) %collective-permute-start.2) | collective-permute-done | bytes 196640 | tf_op jit(solution)/shard_map/ppermute | solution.py:21
  21.6 1.8 %maximum_convert_fusion = f32[8,8,6144]{2,1,0:T(8,128)} fusion(bf16[8,2,6144]{2,1,0:T(2,128)(2,1)S(1)} %collective-permute-done.2, bf16[4,4,6144]{2,1,0:T(4,128)(2,1)S(1)} %bitcast_select_fusion, bf16[4,4,6144]{2,1,0:T(4,128)(2,1)S(1)} %collective-permute-done, bf16[8,2,6144]{2,1,0:T(2,128)(2,1)S(1)} %collective-permute-done.1), kind=kLoop, calls=%fused_computation.26 | loop fusion | flops 3145728 | bytes 2359296 | tf_op jit(solution)/shard_map/convert_element_type | solution.py:27
  23.3 2.2 %reshape.177 = f32[8,8,32,192]{3,2,1,0:T(8,128)S(1)} reshape(f32[8,8,6144]{2,1,0:T(8,128)} %maximum_convert_fusion) | data formatting | bytes 3145728 | tf_op jit(solution)/shard_map/convert_element_type | solution.py:27
  25.5 0.3 multiply_reduce_fusion
  25.9 0.3 copy-done.4
  26.2 0.7 %multiply_convert_fusion = bf16[8,8,32,192]{3,2,1,0:T(8,128)(2,1)S(1)} fusion(f32[8,8,32,192]{3,2,1,0:T(8,128)S(1)} %reshape.177, f32[192]{0:T(256)S(1)} %copy-done.4, f32[8,8,32]{2,1,0:T(8,128)S(1)} %add_rsqrt_fusion), kind=kLoop, calls=%fused_computation.9 | loop fusion | flops 2752512 | bytes 2368256 | tf_op jit(solution)/shard_map/convert_element_type | solution.py:30
  26.9 0.9 %pad_slice_fusion.1 = (bf16[8,8,32,192]{3,2,1,0:T(8,128)(2,1)S(1)}, bf16[8,8,32,192]{3,2,1,0:T(8,128)(2,1)S(1)}) fusion(bf16[8,8,32,192]{3,2,1,0:T(8,128)(2,1)S(1)} %multiply_convert_fusion), kind=kLoop, calls=%fused_computation.13 | loop fusion | bytes 2359296 | tf_op jit(solution)/shard_map/slice | solution.py:39
  27.8 1.1 %pad_maximum_fusion = bf16[8,8,32,576]{3,2,1,0:T(8,128)(2,1)S(1)} fusion(bf16[8,8,32,192]{3,2,1,0:T(8,128)(2,1)S(1)} %get-tuple-element.24, bf16[8,8,32,192]{3,2,1,0:T(8,128)(2,1)S(1)} %multiply_convert_fusion, bf16[8,8,32,192]{3,2,1,0:T(8,128)(2,1)S(1)} %get-tuple-element.23), kind=kLoop, calls=%fused_computation.8 | loop fusion | flops 7077888 | bytes 4718592 | tf_op jit(solution)/shard_map/concatenate | solution.py:37
  28.9 2.0 %fusion.3 = (bf16[6,6,32,576]{3,2,1,0:T(8,128)(2,1)S(1)}, bf16[6,6,32,576]{3,2,1,0:T(8,128)(2,1)S(1)}, bf16[6,6,32,576]{3,2,1,0:T(8,128)(2,1)S(1)}, bf16[6,6,32,...) fusion(bf16[8,8,32,576]{3,2,1,0:T(8,128)(2,1)S(1)} %pad_maximum, ...), kind=kLoop, calls=%fused_computation.61 | loop fusion | bytes 23887872 | tf_op jit(solution)/shard_map/slice | solution.py:49
  31.0 0.6 %fusion.1 = f32[1152,192]{0,1:T(8,128)S(1)} fusion(bf16[1152,576]{1,0:T(8,128)(2,1)S(1)} %bitcast.108, bf16[3,3,576,192]{3,2,1,0:T(8,128)(2,1)S(1)} %bitcast.110), kind=kOutput, calls=%fused_computation.51 | convolution fusion | flops 254803968 | bytes 2654208 | tf_op jit(solution)/shard_map/dot_general | solution.py:52
  31.6 0.7 %convolution_add_fusion.7 = f32[1152,192]{0,1:T(8,128)S(1)} fusion(f32[1152,192]{0,1:T(8,128)S(1)} %fusion.1, bf16[1152,576]{1,0:T(8,128)(2,1)S(1)} %bitcast.107, bf16[3,3,576,192]{3,2,1,0:T(8,128)(2,1)S(1)} %bitcast.111), kind=kOutput, calls=%fused_computation.7 | convolution fusion | flops 255025152 | bytes 3538944 | tf_op jit(solution)/shard_map/dot_general | solution.py:52
  32.3 0.6 %convolution_add_fusion.6 = f32[1152,192]{0,1:T(8,128)S(1)} fusion(f32[1152,192]{0,1:T(8,128)S(1)} %convolution_add_fusion.7, bf16[1152,576]{1,0:T(8,128)(2,1)S(1)} %bitcast.106, bf16[3,3,576,192]{3,2,1,0:T(8,128)(2,1)S(1)} %bitcast.112), kind=kOutput, calls=%fused_computation.6 | convolution fusion | flops 255025152 | bytes 3538944 | tf_op jit(solution)/shard_map/dot_general | solution.py:52
  33.0 0.7 %convolution_add_fusion.5 = f32[1152,192]{0,1:T(8,128)S(1)} fusion(f32[1152,192]{0,1:T(8,128)S(1)} %convolution_add_fusion.6, bf16[1152,576]{1,0:T(8,128)(2,1)S(1)} %bitcast.105, bf16[3,3,576,192]{3,2,1,0:T(8,128)(2,1)S(1)} %bitcast.113), kind=kOutput, calls=%fused_computation.5 | convolution fusion | flops 255025152 | bytes 3538944 | tf_op jit(solution)/shard_map/dot_general | solution.py:52
  33.6 0.6 %convolution_add_fusion.4 = f32[1152,192]{0,1:T(8,128)S(1)} fusion(f32[1152,192]{0,1:T(8,128)S(1)} %convolution_add_fusion.5, bf16[1152,576]{1,0:T(8,128)(2,1)S(1)} %bitcast.104, bf16[3,3,576,192]{3,2,1,0:T(8,128)(2,1)S(1)} %bitcast.114), kind=kOutput, calls=%fused_computation.4 | convolution fusion | flops 255025152 | bytes 3538944 | tf_op jit(solution)/shard_map/dot_general | solution.py:52
  34.3 0.7 %convolution_add_fusion.3 = f32[1152,192]{0,1:T(8,128)S(1)} fusion(f32[1152,192]{0,1:T(8,128)S(1)} %convolution_add_fusion.4, bf16[1152,576]{1,0:T(8,128)(2,1)S(1)} %bitcast.103, bf16[3,3,576,192]{3,2,1,0:T(8,128)(2,1)S(1)} %bitcast.115), kind=kOutput, calls=%fused_computation.3 | convolution fusion | flops 255025152 | bytes 3538944 | tf_op jit(solution)/shard_map/dot_general | solution.py:52
  34.9 0.6 %convolution_add_fusion.2 = f32[1152,192]{0,1:T(8,128)S(1)} fusion(f32[1152,192]{0,1:T(8,128)S(1)} %convolution_add_fusion.3, bf16[1152,576]{1,0:T(8,128)(2,1)S(1)} %bitcast.102, bf16[3,3,576,192]{3,2,1,0:T(8,128)(2,1)S(1)} %bitcast.116), kind=kOutput, calls=%fused_computation.2 | convolution fusion | flops 255025152 | bytes 3538944 | tf_op jit(solution)/shard_map/dot_general | solution.py:52
  35.6 0.6 %convolution_add_fusion.1 = f32[1152,192]{0,1:T(8,128)S(1)} fusion(f32[1152,192]{0,1:T(8,128)S(1)} %convolution_add_fusion.2, bf16[1152,576]{1,0:T(8,128)(2,1)S(1)} %bitcast.101, bf16[3,3,576,192]{3,2,1,0:T(8,128)(2,1)S(1)} %bitcast.117), kind=kOutput, calls=%fused_computation.1 | convolution fusion | flops 255025152 | bytes 3538944 | tf_op jit(solution)/shard_map/dot_general | solution.py:52
  36.3 0.7 %multiply_reduce_fusion.1 = (f32[1152]{0:T(1024)S(1)}, f32[1152,192]{0,1:T(8,128)S(1)}) fusion(f32[192]{0:T(256)S(1)} %copy-done.3, pred[1152]{0:T(1024)(128)(4,1)S(1)} %broadcast_in_dim.61, f32[1152,192]{0,1:T(8,128)S(1)} %convolution_add_fusion.1, bf16[1152,576]{1,0:T(8,128)(2,1)S(1)} %bitcast.100, bf16[3,3,576,192]{3,2,1,0:T(8,128)(2,1)S(1)} %bitcast.118), kind=kOutput, calls=%fused_computation.24 | convolution fusion | flops 256351104 | bytes 3546624 | tf_op jit(solution)/shard_map/dot_general | solution.py:52
  37.0 0.4 copy.9
  37.4 0.2 copy-done.5
  37.7 0.5 %multiply_convert_fusion.1 = bf16[6,6,32,192]{3,2,1,0:T(8,128)(2,1)S(1)} fusion(f32[6,6,32,192]{3,2,1,0:T(8,128)S(1)} %bitcast.109, f32[192]{0:T(256)S(1)} %copy-done.5, f32[6,6,32]{2,1,0:T(8,128)S(1)} %rsqrt.21, f32[192]{0:T(256)S(1)} %copy-done.3, pred[6,6]{1,0:T(8,128)(4,1)S(1)} %broadcast_and_fusion), kind=kLoop, calls=%fused_computation.22 | loop fusion | flops 2433024 | bytes 1333284 | tf_op jit(solution)/shard_map/convert_element_type | solution.py:30
  38.1 0.4 pad_slice_fusion.3
  38.5 0.6 %pad_maximum_fusion.1 = bf16[6,6,32,576]{3,2,1,0:T(8,128)(2,1)S(1)} fusion(bf16[6,6,32,192]{3,2,1,0:T(8,128)(2,1)S(1)} %get-tuple-element.26, bf16[6,6,32,192]{3,2,1,0:T(8,128)(2,1)S(1)} %multiply_convert_fusion.1, bf16[6,6,32,192]{3,2,1,0:T(8,128)(2,1)S(1)} %get-tuple-element.25), kind=kLoop, calls=%fused_computation.11 | loop fusion | flops 3981312 | bytes 2654208 | tf_op jit(solution)/shard_map/concatenate | solution.py:37
  39.1 0.7 %fusion.4 = (bf16[4,4,32,576]{3,2,1,0:T(8,128)(2,1)S(1)}, bf16[4,4,32,576]{3,2,1,0:T(8,128)(2,1)S(1)}, bf16[4,4,32,576]{3,2,1,0:T(8,128)(2,1)S(1)}, bf16[4,4,32,...) fusion(bf16[6,6,32,576]{3,2,1,0:T(8,128)(2,1)S(1)} %pad_maximum, ...), kind=kLoop, calls=%fused_computation.62 | loop fusion | bytes 10616832 | tf_op jit(solution)/shard_map/slice | solution.py:49
  39.8 1.1 %copy-done.1 = bf16[3,3,3,192,192]{4,3,2,1,0:T(8,128)(2,1)S(1)} copy-done((bf16[3,3,3,192,192]{4,3,2,1,0:T(8,128)(2,1)S(1)}, bf16[3,3,3,192,192]{4,3,2,1,0:T(8,128)(2,1)}, u32[]{:S(2)}) %copy-start.1) | copy-done | bytes 1990680
  40.9 0.4 fusion
  41.3 0.4 convolution_add_fusion.15
  41.7 0.4 convolution_add_fusion.14
  42.1 0.4 convolution_add_fusion.13
  42.5 0.4 convolution_add_fusion.12
  42.9 0.4 convolution_add_fusion.11
  43.3 0.4 convolution_add_fusion.10
  43.7 0.4 convolution_add_fusion.9
  44.1 0.4 convolution_add_fusion.8
  44.5 0.2 copy.10
  44.7 0.3 reshape.176
  45.0 0.9 %select_convert_fusion.2 = bf16[1,4,4,6144]{3,2,1,0:T(4,128)(2,1)} fusion(f32[1,4,4,6144]{3,2,1,0:T(4,128)S(1)} %reshape.176, f32[6144]{0:T(1024)S(1)} %add.179, bf16[1,4,4,6144]{3,2,1,0:T(4,128)(2,1)S(1)} %copy-done.2, pred[4]{0:T(512)(128)(4,1)S(1)} %add_compare_fusion), kind=kLoop, calls=%fused_computation.31 | loop fusion | flops 589824 | bytes 811012 | tf_op jit(solution)/shard_map/convert_element_type | solution.py:97
  (16 shorter events, 0.2 us)
Async XLA Ops:
  1.8 8.5 %collective-permute-start = (bf16[4,4,6144]{2,1,0:T(4,128)(2,1)S(1)}, bf16[4,4,6144]{2,1,0:T(4,128)(2,1)S(1)}, u32[]{:S(2)}, u32[]{:S(2)}) collective-permute-start(bf16[4,4,6144]{2,1,0:T(4,128)(2,1)S(1)} %bitcast_select_fusion), channel_id=1, source_target_pairs={{0,4},{4,8},{8,12},{1,5},{5,9},{9,13},{2,6},{6,10},{10,14},{3,7},{... | collective-permute-start | bytes 589832 | tf_op jit(solution)/shard_map/ppermute | solution.py:10
  10.6 6.7 %collective-permute-start.1 = (bf16[8,2,6144]{2,1,0:T(2,128)(2,1)S(1)}, bf16[8,2,6144]{2,1,0:T(2,128)(2,1)S(1)}, u32[]{:S(2)}, u32[]{:S(2)}) collective-permute-start(bf16[8,2,6144]{2,1,0:T(2,128)(2,1)S(1)} %get-tuple-element.27), channel_id=1, source_target_pairs={{0,2},{1,3},{4,6},{5,7},{8,10},{9,11},{12,14},{13,15},{16,18},{17,... | collective-permute-start | bytes 589832 | tf_op jit(solution)/shard_map/ppermute | solution.py:20
  14.0 7.6 %collective-permute-start.2 = (bf16[8,2,6144]{2,1,0:T(2,128)(2,1)S(1)}, bf16[8,2,6144]{2,1,0:T(2,128)(2,1)S(1)}, u32[]{:S(2)}, u32[]{:S(2)}) collective-permute-start(bf16[8,2,6144]{2,1,0:T(2,128)(2,1)S(1)} %get-tuple-element.28), channel_id=1, source_target_pairs={{2,0},{3,1},{6,4},{7,5},{10,8},{11,9},{14,12},{15,13},{18,16},{19,... | collective-permute-start | bytes 589832 | tf_op jit(solution)/shard_map/ppermute | solution.py:21
  25.5 0.7 %copy-start.4 = (f32[192]{0:T(256)S(1)}, f32[192]{0:T(256)}, u32[]{:S(2)}) copy-start(f32[192]{0:T(256)} %param.10) | copy-start | bytes 2308
  28.9 2.1 %copy-start = (bf16[3,3,3,192,192]{4,3,2,1,0:T(8,128)(2,1)S(1)}, bf16[3,3,3,192,192]{4,3,2,1,0:T(8,128)(2,1)}, u32[]{:S(2)}) copy-start(bf16[3,3,3,192,192]{4,3,2,1,0:T(8,128)(2,1)} %param.12) | copy-start | bytes 5971972
  35.6 0.7 %copy-start.3 = (f32[192]{0:T(256)S(1)}, f32[192]{0:T(256)}, u32[]{:S(2)}) copy-start(f32[192]{0:T(256)} %param.11) | copy-start | bytes 2308
  37.0 0.7 %copy-start.5 = (f32[192]{0:T(256)S(1)}, f32[192]{0:T(256)}, u32[]{:S(2)}) copy-start(f32[192]{0:T(256)} %param.13) | copy-start | bytes 2308
  39.1 1.8 %copy-start.1 = (bf16[3,3,3,192,192]{4,3,2,1,0:T(8,128)(2,1)S(1)}, bf16[3,3,3,192,192]{4,3,2,1,0:T(8,128)(2,1)}, u32[]{:S(2)}) copy-start(bf16[3,3,3,192,192]{4,3,2,1,0:T(8,128)(2,1)} %param.15) | copy-start | bytes 5971972
  44.0 0.9 %copy-start.2 = (bf16[1,4,4,6144]{3,2,1,0:T(4,128)(2,1)S(1)}, bf16[1,4,4,6144]{3,2,1,0:T(4,128)(2,1)}, u32[]{:S(2)}) copy-start(bf16[1,4,4,6144]{3,2,1,0:T(4,128)(2,1)} %param.8) | copy-start | bytes 589828
where the time goes:
time: 46.8 us; the launch traced here: 45.9 us
  waiting for transfers between devices  10.3 us (22%)
  local copies, waits for them, and re-layouts  9.67 us (21%)
  matrix products  9.38 us (20%)
  starting transfers between devices  8.18 us (17%)
  other arithmetic  7.37 us (16%)
  between operations  1.03 us (2%)
    dot_general x18, matrix products, conv_local(): jnp.dot(patch_rows.reshape(-1, 3 * channels), merged[shift_time, shift_ro...  9.38 us
    ppermute x1, waiting for transfers between devices, from_behind(): return lax.ppermute(x, axis, pairs)  5 us
    ppermute x1, waiting for transfers between devices, padded_2(): after = lax.ppermute(first, axis, down)  4.3 us
    ppermute x1, starting transfers between devices, from_behind(): return lax.ppermute(x, axis, pairs)  3.48 us
    ppermute x1, starting transfers between devices, padded_2(): before = lax.ppermute(last, axis, up)  3.41 us
    slice x2, local copies, waits for them, and re-layouts, conv_local(): stacked[shift_time:shift_time + out_frames, shift_row:shift_row + out_rows]  2.72 us
    convert_element_type x1, local copies, waits for them, and re-layouts, norm_silu(): values = values.astype(jnp.float32)  2.18 us
    convert_element_type x1, other arithmetic, norm_silu(): values = values.astype(jnp.float32)  1.76 us
  transfers between devices with their start and end apart: 3, of which 3 were waited for; matrix products, arithmetic and copies ran while one was open for 2% of the time, Pallas kernels for 0%

commit v1 on v0

v1 whole, which is shorter than its diff:
```python
import functools

import jax
import jax.numpy as jnp
from jax import lax
from jax.experimental import pallas as pl
from jax.experimental.pallas import tpu as pltpu
from jax.sharding import PartitionSpec as P

MESH = pl.DeviceIdType.MESH
WIDE = 256


def pair_norm(values, valid, gain):
    channels = gain.shape[-1]
    mean_square = jnp.sum(values * values, axis=-1, keepdims=True) * (1.0 / channels)
    scaled = values * lax.rsqrt(mean_square + 1e-06) * gain
    out = scaled * jax.nn.sigmoid(scaled)
    return jnp.where(valid, out, 0.0)


def split_pair(flat, channels):
    return flat[..., :channels], flat[..., channels:]


def kernel(
    bands,
    blocks,
    counts_ref,
    x_ref,
    gain1_ref,
    bias1_ref,
    gain2_ref,
    bias2_ref,
    w1_ref,
    w2_ref,
    out_ref,
    w1,
    w2,
    p1,
    p2,
    from_time,
    from_space,
    from_corner,
    hidden_out,
    hidden_in,
    w_sems,
    send_sems,
    recv_sems,
):
    frames, rows, pairs, flat = x_ref.shape
    channels = flat // 2
    sides = 1 if bands == 2 else 2
    extra = sides
    hrows = rows + extra
    tm = lax.axis_index("tm")
    band = lax.axis_index("space")
    has_prev = tm > 0
    has_next = tm < blocks - 1
    count = counts_ref[0]
    if sides == 1:
        other = 1 - band
        links = [(other, None, other * (rows - 2), 0)]
        own_at = 1 + band
        slot_at = [(1 - band) * (rows + 1)]
        hidden_at = 1 - band
    else:
        links = [
            (band - 1, band > 0, 0, 1),
            (band + 1, band < bands - 1, rows - 2, 0),
        ]
        own_at = 2
        slot_at = [0, rows + 2]
        hidden_at = 0

    def both(a, b):
        return b if a is None else (a if b is None else jnp.logical_and(a, b))

    def when(cond, fn):
        if cond is None:
            fn()
        else:
            pl.when(cond)(fn)

    peers = [({"space": p}, c) for p, c, _, _ in links]
    for step, has in ((1, has_next), (-1, has_prev)):
        peers.append(({"tm": tm + step}, has))
        peers += [({"tm": tm + step, "space": p}, both(c, has)) for p, c, _, _ in links]

    barrier = pltpu.get_barrier_semaphore()
    total = 0
    for device, cond in peers:
        when(
            cond,
            lambda device=device: pl.semaphore_signal(
                barrier, inc=1, device_id=device, device_id_type=MESH
            ),
        )
        total = total + (1 if cond is None else cond.astype(jnp.int32))

    load1 = pltpu.make_async_copy(w1_ref, w1.at[:, pl.ds(0, channels)], w_sems.at[0])
    load2 = pltpu.make_async_copy(w2_ref, w2.at[:, pl.ds(0, channels)], w_sems.at[1])
    load1.start()
    load2.start()

    pl.semaphore_wait(barrier, total)

    tail = pl.ds(frames - 2, 2)
    copies = []

    def remote(src, dst, at, device, send_if, recv_if):
        copy = pltpu.make_async_remote_copy(
            src_ref=src,
            dst_ref=dst,
            send_sem=send_sems.at[at],
            recv_sem=recv_sems.at[at],
            device_id=device,
            device_id_type=MESH,
        )
        return copy, send_if, recv_if

    slot_cond = [None] if sides == 1 else [band > 0, band < bands - 1]
    space_copies, corner_copies = [], []
    for peer, cond, edge, slot in links:
        space_copies.append(
            remote(
                x_ref.at[:, pl.ds(edge, 2)], from_space.at[slot], slot, {"space": peer}, cond, None
            )
        )
        corner_copies.append(
            remote(
                x_ref.at[tail, pl.ds(edge, 2)],
                from_corner.at[slot],
                2 + slot,
                {"tm": tm + 1, "space": peer},
                both(cond, has_next),
                None,
            )
        )
    time_copy = remote(x_ref.at[tail], from_time, 4, {"tm": tm + 1}, has_next, has_prev)
    hidden_copy = remote(hidden_out, hidden_in, 5, {"tm": tm + 1}, has_next, has_prev)
    for copy, cond, _ in space_copies + [time_copy] + corner_copies:
        when(cond, copy.start)

    p1[...] = jnp.zeros_like(p1)
    p2[...] = jnp.zeros_like(p2)
    spare = WIDE - channels
    w1[:, channels:] = jnp.zeros((w1.shape[0], spare, channels), w1.dtype)
    w2[:, channels:] = jnp.zeros((w2.shape[0], spare, channels), w2.dtype)

    first = tm * frames
    pair_index = lax.broadcasted_iota(jnp.int32, (1, 1, pairs, 1), 2)

    def put(planes, even, odd, frame_at, row_at):
        nf, nr = even.shape[:2]
        before = jnp.where(pair_index > 0, pltpu.roll(odd, 1, 2), 0.0)
        after = jnp.where(pair_index < pairs - 1, pltpu.roll(even, pairs - 1, 2), 0.0)
        for plane, values in enumerate((before, even, odd, after)):
            planes[plane, pl.ds(frame_at, nf), pl.ds(row_at, nr), :, pl.ds(0, channels)] = (
                values.astype(planes.dtype)
            )

    def frame_valid(shape, frame_at):
        index = first - 2 + frame_at + lax.broadcasted_iota(jnp.int32, shape, 0)
        return index < count

    def put_input(raw, frame_at, row_at):
        nf, nr = raw.shape[:2]
        even, odd = split_pair(raw.astype(jnp.float32), channels)
        valid = frame_valid((nf, 1, 1, 1), frame_at)
        gain = gain1_ref[...].reshape(1, 1, 1, channels)
        put(p1, pair_norm(even, valid, gain), pair_norm(odd, valid, gain), frame_at, row_at)

    def conv(planes, w, frame_at, nf, nr):
        total = None
        for a in range(3):
            for b in range(3):
                for e in range(3):
                    patch = planes[
                        e : e + 2, frame_at + a : frame_at + a + nf, b : b + nr
                    ].reshape(2 * nf * nr * pairs, WIDE)
                    term = jnp.dot(
                        patch, w[(a * 3 + b) * 3 + e], preferred_element_type=jnp.float32
                    )
                    total = term if total is None else total + term
        return total.reshape(2, nf, nr, pairs, channels)

    def hidden(frame_at, nf):
        summed = conv(p1, w1, frame_at, nf, hrows) + bias1_ref[...].reshape(1, 1, 1, 1, channels)
        valid = frame_valid((nf, 1, 1, 1), frame_at + 2)
        if sides == 2:
            row = band * rows - 1 + lax.broadcasted_iota(jnp.int32, (1, hrows, 1, 1), 1)
            valid = valid & (row >= 0) & (row < bands * rows)
        rounded = summed.astype(jnp.bfloat16).astype(jnp.float32)
        gain = gain2_ref[...].reshape(1, 1, 1, channels)
        even = pair_norm(rounded[0], valid, gain)
        odd = pair_norm(rounded[1], valid, gain)
        put(p2, even, odd, frame_at + 2, hidden_at)
        return even, odd

    def finish(frame_at, nf):
        summed = conv(p2, w2, frame_at, nf, rows) + bias2_ref[...].reshape(1, 1, 1, 1, channels)
        joined = jnp.concatenate([summed[0], summed[1]], axis=-1)
        added = joined + x_ref[pl.ds(frame_at, nf)].astype(jnp.float32)
        valid = frame_valid((nf, 1, 1, 1), frame_at + 2)
        out_ref[pl.ds(frame_at, nf)] = jnp.where(valid, added, 0.0).astype(out_ref.dtype)

    put_input(x_ref[...], 2, own_at)
    for slot, (copy, _, _) in enumerate(space_copies):

        def arrived(slot=slot):
            landed = remote(
                x_ref.at[:, pl.ds(0, 2)], from_space.at[slot], slot, {"space": band}, None, None
            )[0]
            landed.wait_recv()
            put_input(from_space[slot], 2, slot_at[slot])

        when(slot_cond[slot], arrived)

    load1.wait()
    even, odd = hidden(frames - 2, 2)
    hidden_out[0] = even.astype(hidden_out.dtype)
    hidden_out[1] = odd.astype(hidden_out.dtype)
    when(has_next, hidden_copy[0].start)

    def time_arrived():
        time_copy[0].wait_recv()
        put_input(from_time[...], 0, own_at)

    when(has_prev, time_arrived)
    for slot in range(sides):

        def corner_arrived(slot=slot):
            landed = remote(
                x_ref.at[tail, pl.ds(0, 2)],
                from_corner.at[slot],
                2 + slot,
                {"space": band},
                None,
                None,
            )[0]
            landed.wait_recv()
            put_input(from_corner[slot], 0, slot_at[slot])

        when(both(slot_cond[slot], has_prev), corner_arrived)

    hidden(0, frames - 2)
    load2.wait()
    finish(frames - 2, 2)

    def hidden_arrived():
        hidden_copy[0].wait_recv()
        even = hidden_in[0].astype(jnp.float32)
        odd = hidden_in[1].astype(jnp.float32)
        put(p2, even, odd, 0, hidden_at)

    when(has_prev, hidden_arrived)
    finish(0, frames - 2)
    for copy, cond, _ in space_copies + corner_copies + [time_copy, hidden_copy]:
        when(cond, copy.wait_send)


def shards(
    bands,
    blocks,
    latents,
    frame_counts,
    gain_first,
    bias_first,
    weight_first,
    gain_second,
    bias_second,
    weight_second,
):
    channels = gain_first.shape[0]
    frames, rows, flat_width = latents.shape[1:]
    pairs = flat_width // (2 * channels)
    x = latents.reshape(frames, rows, pairs, 2 * channels)
    sides = 1 if bands == 2 else 2
    hrows = rows + sides
    bf16 = jnp.bfloat16
    vmem = pl.BlockSpec(memory_space=pltpu.VMEM)
    hbm = pl.BlockSpec(memory_space=pl.ANY)
    out = pl.pallas_call(
        functools.partial(kernel, bands, blocks),
        out_shape=jax.ShapeDtypeStruct(x.shape, bf16),
        in_specs=[pl.BlockSpec(memory_space=pltpu.SMEM)] + [vmem] * 5 + [hbm] * 2,
        out_specs=vmem,
        scratch_shapes=[
            pltpu.VMEM((27, WIDE, channels), bf16),
            pltpu.VMEM((27, WIDE, channels), bf16),
            pltpu.VMEM((4, frames + 2, hrows + 2, pairs, WIDE), bf16),
            pltpu.VMEM((4, frames + 2, rows + 2, pairs, WIDE), bf16),
            pltpu.VMEM((2, rows, pairs, 2 * channels), bf16),
            pltpu.VMEM((sides, frames, 2, pairs, 2 * channels), bf16),
            pltpu.VMEM((sides, 2, 2, pairs, 2 * channels), bf16),
            pltpu.VMEM((2, 2, hrows, pairs, channels), bf16),
            pltpu.VMEM((2, 2, hrows, pairs, channels), bf16),
            pltpu.SemaphoreType.DMA((2,)),
            pltpu.SemaphoreType.DMA((6,)),
            pltpu.SemaphoreType.DMA((6,)),
        ],
        compiler_params=pltpu.CompilerParams(
            collective_id=0, has_side_effects=True, vmem_limit_bytes=40 * 1024 * 1024
        ),
    )(
        frame_counts,
        x,
        gain_first.reshape(1, channels),
        bias_first.reshape(1, channels),
        gain_second.reshape(1, channels),
        bias_second.reshape(1, channels),
        weight_first.reshape(27, channels, channels),
        weight_second.reshape(27, channels, channels),
    )
    return out.reshape(latents.shape)


def solution(mesh):
    return jax.shard_map(
        functools.partial(shards, mesh.shape["space"], mesh.shape["tm"]),
        mesh=mesh,
        in_specs=(P(("groups", "clip"), "tm", "space", None), P(("groups", "clip"))) + (P(),) * 6,
        out_specs=P(("groups", "clip"), "tm", "space", None),
        check_vma=False,
    )
```

time: 46.8 us -> 25.9 us (0.55); the launches traced: 45.9 us -> 25.6 us
  Pallas kernels: 0 us -> 16.9 us
  waiting for transfers between devices: 10.3 us -> 0 us
  matrix products: 9.38 us -> 0 us
  starting transfers between devices: 8.18 us -> 0 us
  other arithmetic: 7.37 us -> 0 us
  local copies, waits for them, and re-layouts: 9.67 us -> 7.99 us
    pallas_call x0 -> x1, Pallas kernels: none -> 16.9 us  [shards(): pl.pallas_call(functools.partial(kernel, bands, blocks), out_shape=jax.Sh...]
    ppermute x3 -> x0, waiting for transfers between devices: 10.3 us -> none  [the longest x1 5 us: from_behind(): return lax.ppermute(x, axis, pairs)]
    dot_general x18 -> x0, matrix products: 9.38 us -> none  [conv_local(): jnp.dot(patch_rows.reshape(-1, 3 * channels), merged[shift_time, shift_ro...]
    ppermute x3 -> x0, starting transfers between devices: 8.18 us -> none  [the longest x1 3.48 us: from_behind(): return lax.ppermute(x, axis, pairs)]
    unnamed x12, local copies, waits for them, and re-layouts: 1.61 us -> 6.21 us
    slice x4 -> x0, local copies, waits for them, and re-layouts: 3.99 us -> none  [the longest x2 2.72 us: conv_local(): stacked[shift_time:shift_time + out_frames, shift_row:shift_row + out_rows]]
    convert_element_type x4 -> x0, other arithmetic: 3.79 us -> none  [the longest x1 1.76 us: norm_silu(): values = values.astype(jnp.float32)]
    convert_element_type x1 -> x0, local copies, waits for them, and re-layouts: 2.18 us -> none  [norm_silu(): values = values.astype(jnp.float32)]
  transfers between devices with their start and end apart: 3 -> 0, of which waited for: 3 -> 0; matrix products, arithmetic and copies ran while one was open for 2% -> 0% of each run, Pallas kernels for 0% -> 0%
where the time goes in v1:
time: 25.9 us; the launch traced here: 25.6 us
  Pallas kernels  16.9 us (65%)
  local copies, waits for them, and re-layouts  7.99 us (31%)
  between operations  0.68 us (3%)
    pallas_call x1, Pallas kernels, shards(): pl.pallas_call(functools.partial(kernel, bands, blocks), out_shape=jax.Sh...  16.9 us
    unnamed x12, local copies, waits for them, and re-layouts  6.21 us
    reshape x1, local copies, waits for them, and re-layouts, shards(): x = latents.reshape(frames, rows, pairs, 2 * channels)  1.05 us
    reshape x1, local copies, waits for them, and re-layouts, shards(): return out.reshape(latents.shape)  0.73 us

profile of v1, /device:TPU:8, one launch (start us, length us, event | category | flops | bytes accessed | tf_op | source)
XLA Modules:
  0.0 25.6 jit_solution(1965877748036297499)
XLA Ops:
  0.7 1.1 %reshape.24.x_ref = bf16[4,4,16,384]{3,2,1,0:T(8,128)(2,1)S(1)} reshape(bf16[1,4,4,6144]{3,2,1,0:T(4,128)(2,1)} %param.8) | data formatting | bytes 393216 | tf_op jit(solution)/shard_map/reshape | solution.py:278
  1.7 0.0 copy-start
  1.7 1.7 %copy-done = bf16[3,3,3,192,192]{4,3,2,1,0:T(8,128)(2,1)S(1)} copy-done((bf16[3,3,3,192,192]{4,3,2,1,0:T(8,128)(2,1)S(1)}, bf16[3,3,3,192,192]{4,3,2,1,0:T(8,128)(2,1)}, u32[]{:S(2)}) %copy-start) | copy-done | bytes 1990680
  3.5 0.0 copy-start.1
  3.5 1.7 %copy-done.1 = bf16[3,3,3,192,192]{4,3,2,1,0:T(8,128)(2,1)S(1)} copy-done((bf16[3,3,3,192,192]{4,3,2,1,0:T(8,128)(2,1)S(1)}, bf16[3,3,3,192,192]{4,3,2,1,0:T(8,128)(2,1)}, u32[]{:S(2)}) %copy-start.1) | copy-done | bytes 1990680
  5.2 0.0 copy-start.2
  5.2 0.7 %copy-done.2 = f32[192]{0:T(256)S(1)} copy-done((f32[192]{0:T(256)S(1)}, f32[192]{0:T(256)}, u32[]{:S(2)}) %copy-start.2) | copy-done | bytes 792
  5.9 0.0 copy-start.3
  5.9 0.7 %copy-done.3 = f32[192]{0:T(256)S(1)} copy-done((f32[192]{0:T(256)S(1)}, f32[192]{0:T(256)}, u32[]{:S(2)}) %copy-start.3) | copy-done | bytes 792
  6.6 0.0 copy-start.4
  6.6 0.7 %copy-done.4 = f32[192]{0:T(256)S(1)} copy-done((f32[192]{0:T(256)S(1)}, f32[192]{0:T(256)}, u32[]{:S(2)}) %copy-start.4) | copy-done | bytes 792
  7.2 0.0 copy-start.5
  7.3 0.7 %copy-done.5 = f32[192]{0:T(256)S(1)} copy-done((f32[192]{0:T(256)S(1)}, f32[192]{0:T(256)}, u32[]{:S(2)}) %copy-start.5) | copy-done | bytes 792
  7.9 16.9 %shard_map.82 = bf16[4,4,16,384]{3,2,1,0:T(8,128)(2,1)S(1)} custom-call(s32[1]{0:T(128)S(6)} %copy.9.counts_ref, bf16[4,4,16,384]{3,2,1,0:T(8,128)(2,1)S(1)} %reshape.24.x_ref, f32[1,192]{1,0:T(1,128)S(1)} %bitcast.10, f32[1,192]{1,0:T(1,128)S(1)} %bitcast.11, f32[1,192]{1,0:T(1,128)S(1)} %bitcast.12, f32[1,192]{1,0:T(1,128)S(1)} %bitcast.13, ...), custom_call_target="tpu_custom_call" | custom-call | tf_op jit(solution)/shard_map/pallas_call | solution.py:284
  24.8 0.7 %reshape.31 = bf16[1,4,4,6144]{3,2,1,0:T(4,128)(2,1)} reshape(bf16[4,4,16,384]{3,2,1,0:T(8,128)(2,1)S(1)} %shard_map.82) | data formatting | bytes 393216 | tf_op jit(solution)/shard_map/reshape | solution.py:316
Async XLA Ops:
  1.7 1.8 %copy-start = (bf16[3,3,3,192,192]{4,3,2,1,0:T(8,128)(2,1)S(1)}, bf16[3,3,3,192,192]{4,3,2,1,0:T(8,128)(2,1)}, u32[]{:S(2)}) copy-start(bf16[3,3,3,192,192]{4,3,2,1,0:T(8,128)(2,1)} %param.12) | copy-start | bytes 5971972
  3.5 1.7 %copy-start.1 = (bf16[3,3,3,192,192]{4,3,2,1,0:T(8,128)(2,1)S(1)}, bf16[3,3,3,192,192]{4,3,2,1,0:T(8,128)(2,1)}, u32[]{:S(2)}) copy-start(bf16[3,3,3,192,192]{4,3,2,1,0:T(8,128)(2,1)} %param.15) | copy-start | bytes 5971972
  5.2 0.7 %copy-start.2 = (f32[192]{0:T(256)S(1)}, f32[192]{0:T(256)}, u32[]{:S(2)}) copy-start(f32[192]{0:T(256)} %param.10) | copy-start | bytes 2308
  5.9 0.7 %copy-start.3 = (f32[192]{0:T(256)S(1)}, f32[192]{0:T(256)}, u32[]{:S(2)}) copy-start(f32[192]{0:T(256)} %param.11) | copy-start | bytes 2308
  6.6 0.7 %copy-start.4 = (f32[192]{0:T(256)S(1)}, f32[192]{0:T(256)}, u32[]{:S(2)}) copy-start(f32[192]{0:T(256)} %param.13) | copy-start | bytes 2308
  7.2 0.7 %copy-start.5 = (f32[192]{0:T(256)S(1)}, f32[192]{0:T(256)}, u32[]{:S(2)}) copy-start(f32[192]{0:T(256)} %param.14) | copy-start | bytes 2308

commit v2 on v1

--- a/solution.py
+++ b/solution.py
@@ -28,13 +28,14 @@
     blocks,
     counts_ref,
     x_ref,
-    gain1_ref,
-    bias1_ref,
-    gain2_ref,
-    bias2_ref,
+    gain1_hbm,
+    bias1_hbm,
+    gain2_hbm,
+    bias2_hbm,
     w1_ref,
     w2_ref,
     out_ref,
+    vectors,
     w1,
     w2,
     p1,
@@ -100,6 +101,13 @@
 
     load1 = pltpu.make_async_copy(w1_ref, w1.at[:, pl.ds(0, channels)], w_sems.at[0])
     load2 = pltpu.make_async_copy(w2_ref, w2.at[:, pl.ds(0, channels)], w_sems.at[1])
+    small = [
+        pltpu.make_async_copy(source, vectors.at[i], w_sems.at[2 + i])
+        for i, source in enumerate((gain1_hbm, bias1_hbm, gain2_hbm, bias2_hbm))
+    ]
+    gain1_ref, bias1_ref, gain2_ref, bias2_ref = [vectors.at[i] for i in range(4)]
+    for copy in small:
+        copy.start()
     load1.start()
     load2.start()
 
@@ -205,6 +213,8 @@
         valid = frame_valid((nf, 1, 1, 1), frame_at + 2)
         out_ref[pl.ds(frame_at, nf)] = jnp.where(valid, added, 0.0).astype(out_ref.dtype)
 
+    for copy in small:
+        copy.wait()
     put_input(x_ref[...], 2, own_at)
     for slot, (copy, _, _) in enumerate(space_copies):
 
@@ -280,13 +290,14 @@
     hrows = rows + sides
     bf16 = jnp.bfloat16
     vmem = pl.BlockSpec(memory_space=pltpu.VMEM)
-    hbm = pl.BlockSpec(memory_space=pl.ANY)
+    hbm = pl.BlockSpec(memory_space=pltpu.HBM)
     out = pl.pallas_call(
         functools.partial(kernel, bands, blocks),
         out_shape=jax.ShapeDtypeStruct(x.shape, bf16),
-        in_specs=[pl.BlockSpec(memory_space=pltpu.SMEM)] + [vmem] * 5 + [hbm] * 2,
+        in_specs=[pl.BlockSpec(memory_space=pltpu.SMEM)] + [vmem] + [hbm] * 6,
         out_specs=vmem,
         scratch_shapes=[
+            pltpu.VMEM((4, 1, channels), jnp.float32),
             pltpu.VMEM((27, WIDE, channels), bf16),
             pltpu.VMEM((27, WIDE, channels), bf16),
             pltpu.VMEM((4, frames + 2, hrows + 2, pairs, WIDE), bf16),
@@ -296,12 +307,12 @@
             pltpu.VMEM((sides, 2, 2, pairs, 2 * channels), bf16),
             pltpu.VMEM((2, 2, hrows, pairs, channels), bf16),
             pltpu.VMEM((2, 2, hrows, pairs, channels), bf16),
-            pltpu.SemaphoreType.DMA((2,)),
+            pltpu.SemaphoreType.DMA((6,)),
             pltpu.SemaphoreType.DMA((6,)),
             pltpu.SemaphoreType.DMA((6,)),
         ],
         compiler_params=pltpu.CompilerParams(
-            collective_id=0, has_side_effects=True, vmem_limit_bytes=40 * 1024 * 1024
+            collective_id=0, has_side_effects=True, vmem_limit_bytes=61 * 1024 * 1024
         ),
     )(
         frame_counts,

time: 25.9 us -> 22.8 us (0.88)
  local copies, waits for them, and re-layouts: 7.99 us -> 3.38 us
  Pallas kernels: 16.9 us -> 18.5 us
    unnamed x12 -> x0, local copies, waits for them, and re-layouts: 6.21 us -> none
    pallas_call x1, Pallas kernels: 16.9 us -> 18.5 us  [shards(): pl.pallas_call(functools.partial(kernel, bands, blocks), out_shape=jax.Sh...]
    reshape x1, local copies, waits for them, and re-layouts: 0.73 us -> 1.65 us  [shards(): return out.reshape(latents.shape)]
    reshape x1, local copies, waits for them, and re-layouts: 1.05 us -> 1.73 us  [shards(): x = latents.reshape(frames, rows, pairs, 2 * channels)]
where the time goes in v2:
time: 22.8 us; the launch traced here: 22.6 us
  Pallas kernels  18.5 us (81%)
  local copies, waits for them, and re-layouts  3.38 us (15%)
  between operations  0.66 us (3%)
    pallas_call x1, Pallas kernels, shards(): pl.pallas_call(functools.partial(kernel, bands, blocks), out_shape=jax.Sh...  18.5 us
    reshape x1, local copies, waits for them, and re-layouts, shards(): x = latents.reshape(frames, rows, pairs, 2 * channels)  1.73 us
    reshape x1, local copies, waits for them, and re-layouts, shards(): return out.reshape(latents.shape)  1.65 us

profile of v2, /device:TPU:8, one launch (start us, length us, event | category | flops | bytes accessed | tf_op | source)
XLA Modules:
  0.0 22.6 jit_solution(12972807305362430001)
XLA Ops:
  0.7 1.7 %reshape.24.x_ref = bf16[4,4,16,384]{3,2,1,0:T(8,128)(2,1)} reshape(bf16[1,4,4,6144]{3,2,1,0:T(4,128)(2,1)} %param.8) | data formatting | bytes 393216 | tf_op jit(solution)/shard_map/reshape | solution.py:288
  2.4 18.5 %shard_map.82 = bf16[4,4,16,384]{3,2,1,0:T(8,128)(2,1)} custom-call(s32[1]{0:T(128)S(6)} %copy.9.counts_ref, bf16[4,4,16,384]{3,2,1,0:T(8,128)(2,1)} %reshape.24.x_ref, f32[1,192]{1,0:T(1,128)} %bitcast.10, f32[1,192]{1,0:T(1,128)} %bitcast.11, f32[1,192]{1,0:T(1,128)} %bitcast.12, f32[1,192]{1,0:T(1,128)} %bitcast.13, bf16[27,192,192]{2,1,0:T(8,128)(2,1)} %bitcast.8, ...), custom_call_target="tpu_custom_call" | custom-call | tf_op jit(solution)/shard_map/pallas_call | solution.py:294
  20.9 1.7 %reshape.31 = bf16[1,4,4,6144]{3,2,1,0:T(4,128)(2,1)} reshape(bf16[4,4,16,384]{3,2,1,0:T(8,128)(2,1)} %shard_map.82) | data formatting | bytes 393216 | tf_op jit(solution)/shard_map/reshape | solution.py:327

commit v3 on v2

--- a/solution.py
+++ b/solution.py
@@ -111,6 +111,12 @@
     load1.start()
     load2.start()
 
+    p1[...] = jnp.zeros_like(p1)
+    p2[...] = jnp.zeros_like(p2)
+    spare = WIDE - channels
+    w1[:, channels:] = jnp.zeros((w1.shape[0], spare, channels), w1.dtype)
+    w2[:, channels:] = jnp.zeros((w2.shape[0], spare, channels), w2.dtype)
+
     pl.semaphore_wait(barrier, total)
 
     tail = pl.ds(frames - 2, 2)
@@ -150,12 +156,6 @@
     for copy, cond, _ in space_copies + [time_copy] + corner_copies:
         when(cond, copy.start)
 
-    p1[...] = jnp.zeros_like(p1)
-    p2[...] = jnp.zeros_like(p2)
-    spare = WIDE - channels
-    w1[:, channels:] = jnp.zeros((w1.shape[0], spare, channels), w1.dtype)
-    w2[:, channels:] = jnp.zeros((w2.shape[0], spare, channels), w2.dtype)
-
     first = tm * frames
     pair_index = lax.broadcasted_iota(jnp.int32, (1, 1, pairs, 1), 2)
 
@@ -229,8 +229,7 @@
 
     load1.wait()
     even, odd = hidden(frames - 2, 2)
-    hidden_out[0] = even.astype(hidden_out.dtype)
-    hidden_out[1] = odd.astype(hidden_out.dtype)
+    hidden_out[...] = jnp.concatenate([even, odd], axis=-1).astype(hidden_out.dtype)
     when(has_next, hidden_copy[0].start)
 
     def time_arrived():
@@ -260,8 +259,7 @@
 
     def hidden_arrived():
         hidden_copy[0].wait_recv()
-        even = hidden_in[0].astype(jnp.float32)
-        odd = hidden_in[1].astype(jnp.float32)
+        even, odd = split_pair(hidden_in[...].astype(jnp.float32), channels)
         put(p2, even, odd, 0, hidden_at)
 
     when(has_prev, hidden_arrived)
@@ -293,7 +291,7 @@
     hbm = pl.BlockSpec(memory_space=pltpu.HBM)
     out = pl.pallas_call(
         functools.partial(kernel, bands, blocks),
-        out_shape=jax.ShapeDtypeStruct(x.shape, bf16),
+        out_shape=pltpu.VMEM(x.shape, bf16),
         in_specs=[pl.BlockSpec(memory_space=pltpu.SMEM)] + [vmem] + [hbm] * 6,
         out_specs=vmem,
         scratch_shapes=[
@@ -305,24 +303,24 @@
             pltpu.VMEM((2, rows, pairs, 2 * channels), bf16),
             pltpu.VMEM((sides, frames, 2, pairs, 2 * channels), bf16),
             pltpu.VMEM((sides, 2, 2, pairs, 2 * channels), bf16),
-            pltpu.VMEM((2, 2, hrows, pairs, channels), bf16),
-            pltpu.VMEM((2, 2, hrows, pairs, channels), bf16),
+            pltpu.VMEM((2, hrows, pairs, 2 * channels), bf16),
+            pltpu.VMEM((2, hrows, pairs, 2 * channels), bf16),
             pltpu.SemaphoreType.DMA((6,)),
             pltpu.SemaphoreType.DMA((6,)),
             pltpu.SemaphoreType.DMA((6,)),
         ],
         compiler_params=pltpu.CompilerParams(
-            collective_id=0, has_side_effects=True, vmem_limit_bytes=61 * 1024 * 1024
+            collective_id=0, has_side_effects=True, vmem_limit_bytes=40 * 1024 * 1024
         ),
     )(
         frame_counts,
-        x,
-        gain_first.reshape(1, channels),
-        bias_first.reshape(1, channels),
-        gain_second.reshape(1, channels),
-        bias_second.reshape(1, channels),
-        weight_first.reshape(27, channels, channels),
-        weight_second.reshape(27, channels, channels),
+        pltpu.with_memory_space_constraint(x, pltpu.VMEM),
+        pltpu.with_memory_space_constraint(gain_first.reshape(1, channels), pltpu.HBM),
+        pltpu.with_memory_space_constraint(bias_first.reshape(1, channels), pltpu.HBM),
+        pltpu.with_memory_space_constraint(gain_second.reshape(1, channels), pltpu.HBM),
+        pltpu.with_memory_space_constraint(bias_second.reshape(1, channels), pltpu.HBM),
+        pltpu.with_memory_space_constraint(weight_first.reshape(27, channels, channels), pltpu.HBM),
+        pltpu.with_memory_space_constraint(weight_second.reshape(27, channels, channels), pltpu.HBM),
     )
     return out.reshape(latents.shape)
 

time: 22.8 us -> 19.7 us (0.86)
  local copies, waits for them, and re-layouts: 3.38 us -> 1.78 us
  Pallas kernels: 18.5 us -> 17.2 us
    pallas_call x1, Pallas kernels: 18.5 us -> 17.2 us  [shards(): pl.pallas_call(functools.partial(kernel, bands, blocks), out_shape=pltpu....]
    reshape x1, local copies, waits for them, and re-layouts: 1.65 us -> 0.73 us  [shards(): return out.reshape(latents.shape)]
    reshape x1, local copies, waits for them, and re-layouts: 1.73 us -> 1.05 us  [shards(): x = latents.reshape(frames, rows, pairs, 2 * channels)]
where the time goes in v3:
time: 19.7 us; the launch traced here: 19.6 us
  Pallas kernels  17.2 us (87%)
  local copies, waits for them, and re-layouts  1.78 us (9%)
  between operations  0.66 us (3%)
    pallas_call x1, Pallas kernels, shards(): pl.pallas_call(functools.partial(kernel, bands, blocks), out_shape=pltpu....  17.2 us
    reshape x1, local copies, waits for them, and re-layouts, shards(): x = latents.reshape(frames, rows, pairs, 2 * channels)  1.05 us
    reshape x1, local copies, waits for them, and re-layouts, shards(): return out.reshape(latents.shape)  0.73 us

profile of v3, /device:TPU:8, one launch (start us, length us, event | category | flops | bytes accessed | tf_op | source)
XLA Modules:
  0.0 19.6 jit_solution(18265591640506324497)
XLA Ops:
  0.7 1.1 %reshape.24.x_ref = bf16[4,4,16,384]{3,2,1,0:T(8,128)(2,1)S(1)} reshape(bf16[1,4,4,6144]{3,2,1,0:T(4,128)(2,1)} %param.8) | data formatting | bytes 393216 | tf_op jit(solution)/shard_map/reshape | solution.py:286
  1.7 17.2 %shard_map.82 = bf16[4,4,16,384]{3,2,1,0:T(8,128)(2,1)S(1)} custom-call(s32[1]{0:T(128)S(6)} %copy.9.counts_ref, bf16[4,4,16,384]{3,2,1,0:T(8,128)(2,1)S(1)} %reshape.24.x_ref, f32[1,192]{1,0:T(1,128)} %bitcast.10, f32[1,192]{1,0:T(1,128)} %bitcast.11, f32[1,192]{1,0:T(1,128)} %bitcast.12, f32[1,192]{1,0:T(1,128)} %bitcast.13, ...), custom_call_target="tpu_custom_call" | custom-call | tf_op jit(solution)/shard_map/pallas_call | solution.py:292
  18.9 0.7 %reshape.31 = bf16[1,4,4,6144]{3,2,1,0:T(4,128)(2,1)} reshape(bf16[4,4,16,384]{3,2,1,0:T(8,128)(2,1)S(1)} %shard_map.82) | data formatting | bytes 393216 | tf_op jit(solution)/shard_map/reshape | solution.py:325

commit v4 on v3

--- a/solution.py
+++ b/solution.py
@@ -179,13 +179,13 @@
         gain = gain1_ref[...].reshape(1, 1, 1, channels)
         put(p1, pair_norm(even, valid, gain), pair_norm(odd, valid, gain), frame_at, row_at)
 
-    def conv(planes, w, frame_at, nf, nr):
+    def conv(planes, w, frame_at, nf, nr, row_at=0):
         total = None
         for a in range(3):
             for b in range(3):
                 for e in range(3):
                     patch = planes[
-                        e : e + 2, frame_at + a : frame_at + a + nf, b : b + nr
+                        e : e + 2, frame_at + a : frame_at + a + nf, pl.ds(row_at + b, nr)
                     ].reshape(2 * nf * nr * pairs, WIDE)
                     term = jnp.dot(
                         patch, w[(a * 3 + b) * 3 + e], preferred_element_type=jnp.float32
@@ -193,8 +193,8 @@
                     total = term if total is None else total + term
         return total.reshape(2, nf, nr, pairs, channels)
 
-    def hidden(frame_at, nf):
-        summed = conv(p1, w1, frame_at, nf, hrows) + bias1_ref[...].reshape(1, 1, 1, 1, channels)
+    def hidden(frame_at, nf, nr=hrows, row_at=0):
+        summed = conv(p1, w1, frame_at, nf, nr, row_at) + bias1_ref[...].reshape(1, 1, 1, 1, channels)
         valid = frame_valid((nf, 1, 1, 1), frame_at + 2)
         if sides == 2:
             row = band * rows - 1 + lax.broadcasted_iota(jnp.int32, (1, hrows, 1, 1), 1)
@@ -203,8 +203,8 @@
         gain = gain2_ref[...].reshape(1, 1, 1, channels)
         even = pair_norm(rounded[0], valid, gain)
         odd = pair_norm(rounded[1], valid, gain)
-        put(p2, even, odd, frame_at + 2, hidden_at)
-        return even, odd
+        put(p2, even, odd, frame_at + 2, hidden_at + row_at)
+        return jnp.concatenate([even, odd], axis=-1).astype(hidden_out.dtype)
 
     def finish(frame_at, nf):
         summed = conv(p2, w2, frame_at, nf, rows) + bias2_ref[...].reshape(1, 1, 1, 1, channels)
@@ -216,6 +216,10 @@
     for copy in small:
         copy.wait()
     put_input(x_ref[...], 2, own_at)
+    load1.wait()
+    if sides == 1:
+        near = rows - 1
+        hidden_out[:, pl.ds(2 * band, near)] = hidden(frames - 2, 2, near, 2 * band)
     for slot, (copy, _, _) in enumerate(space_copies):
 
         def arrived(slot=slot):
@@ -227,9 +231,11 @@
 
         when(slot_cond[slot], arrived)
 
-    load1.wait()
-    even, odd = hidden(frames - 2, 2)
-    hidden_out[...] = jnp.concatenate([even, odd], axis=-1).astype(hidden_out.dtype)
+    if sides == 1:
+        far_at = near * (1 - band)
+        hidden_out[:, pl.ds(far_at, 2)] = hidden(frames - 2, 2, 2, far_at)
+    else:
+        hidden_out[...] = hidden(frames - 2, 2)
     when(has_next, hidden_copy[0].start)
 
     def time_arrived():

time: 19.7 us -> 17.5 us (0.89)
  Pallas kernels: 17.2 us -> 14.9 us
    pallas_call x1, Pallas kernels: 17.2 us -> 14.9 us  [shards(): pl.pallas_call(functools.partial(kernel, bands, blocks), out_shape=pltpu....]
where the time goes in v4:
time: 17.5 us; the launch traced here: 17.3 us
  Pallas kernels  14.9 us (85%)
  local copies, waits for them, and re-layouts  1.78 us (10%)
  between operations  0.66 us (4%)
    pallas_call x1, Pallas kernels, shards(): pl.pallas_call(functools.partial(kernel, bands, blocks), out_shape=pltpu....  14.9 us
    reshape x1, local copies, waits for them, and re-layouts, shards(): x = latents.reshape(frames, rows, pairs, 2 * channels)  1.05 us
    reshape x1, local copies, waits for them, and re-layouts, shards(): return out.reshape(latents.shape)  0.73 us

profile of v4, /device:TPU:8, one launch (start us, length us, event | category | flops | bytes accessed | tf_op | source)
XLA Modules:
  0.0 17.3 jit_solution(6519777912198181531)
XLA Ops:
  0.7 1.1 %reshape.24.x_ref = bf16[4,4,16,384]{3,2,1,0:T(8,128)(2,1)S(1)} reshape(bf16[1,4,4,6144]{3,2,1,0:T(4,128)(2,1)} %param.8) | data formatting | bytes 393216 | tf_op jit(solution)/shard_map/reshape | solution.py:292
  1.7 14.9 %shard_map.82 = bf16[4,4,16,384]{3,2,1,0:T(8,128)(2,1)S(1)} custom-call(s32[1]{0:T(128)S(6)} %copy.9.counts_ref, bf16[4,4,16,384]{3,2,1,0:T(8,128)(2,1)S(1)} %reshape.24.x_ref, f32[1,192]{1,0:T(1,128)} %bitcast.10, f32[1,192]{1,0:T(1,128)} %bitcast.11, f32[1,192]{1,0:T(1,128)} %bitcast.12, f32[1,192]{1,0:T(1,128)} %bitcast.13, ...), custom_call_target="tpu_custom_call" | custom-call | tf_op jit(solution)/shard_map/pallas_call | solution.py:298
  16.6 0.7 %reshape.31 = bf16[1,4,4,6144]{3,2,1,0:T(4,128)(2,1)} reshape(bf16[4,4,16,384]{3,2,1,0:T(8,128)(2,1)S(1)} %shard_map.82) | data formatting | bytes 393216 | tf_op jit(solution)/shard_map/reshape | solution.py:331

commit v5 on v4

--- a/solution.py
+++ b/solution.py
@@ -243,6 +243,8 @@
         put_input(from_time[...], 0, own_at)
 
     when(has_prev, time_arrived)
+    if sides == 1:
+        hidden(0, frames - 2, near, 2 * band)
     for slot in range(sides):
 
         def corner_arrived(slot=slot):
@@ -259,7 +261,10 @@
 
         when(both(slot_cond[slot], has_prev), corner_arrived)
 
-    hidden(0, frames - 2)
+    if sides == 1:
+        hidden(0, frames - 2, 2, far_at)
+    else:
+        hidden(0, frames - 2)
     load2.wait()
     finish(frames - 2, 2)
 

time: 17.5 us -> 18.6 us (1.063)
  Pallas kernels: 14.9 us -> 16 us
    pallas_call x1, Pallas kernels: 14.9 us -> 16 us  [shards(): pl.pallas_call(functools.partial(kernel, bands, blocks), out_shape=pltpu....]
where the time goes in v5:
time: 18.6 us; the launch traced here: 18.5 us
  Pallas kernels  16 us (86%)
  local copies, waits for them, and re-layouts  1.78 us (10%)
  between operations  0.66 us (4%)
    pallas_call x1, Pallas kernels, shards(): pl.pallas_call(functools.partial(kernel, bands, blocks), out_shape=pltpu....  16 us
    reshape x1, local copies, waits for them, and re-layouts, shards(): x = latents.reshape(frames, rows, pairs, 2 * channels)  1.05 us
    reshape x1, local copies, waits for them, and re-layouts, shards(): return out.reshape(latents.shape)  0.73 us

profile of v5, /device:TPU:8, one launch (start us, length us, event | category | flops | bytes accessed | tf_op | source)
XLA Modules:
  0.0 18.5 jit_solution(2907820173641788647)
XLA Ops:
  0.7 1.1 %reshape.24.x_ref = bf16[4,4,16,384]{3,2,1,0:T(8,128)(2,1)S(1)} reshape(bf16[1,4,4,6144]{3,2,1,0:T(4,128)(2,1)} %param.8) | data formatting | bytes 393216 | tf_op jit(solution)/shard_map/reshape | solution.py:297
  1.7 16.0 %shard_map.82 = bf16[4,4,16,384]{3,2,1,0:T(8,128)(2,1)S(1)} custom-call(s32[1]{0:T(128)S(6)} %copy.9.counts_ref, bf16[4,4,16,384]{3,2,1,0:T(8,128)(2,1)S(1)} %reshape.24.x_ref, f32[1,192]{1,0:T(1,128)} %bitcast.10, f32[1,192]{1,0:T(1,128)} %bitcast.11, f32[1,192]{1,0:T(1,128)} %bitcast.12, f32[1,192]{1,0:T(1,128)} %bitcast.13, ...), custom_call_target="tpu_custom_call" | custom-call | tf_op jit(solution)/shard_map/pallas_call | solution.py:303
  17.7 0.7 %reshape.31 = bf16[1,4,4,6144]{3,2,1,0:T(4,128)(2,1)} reshape(bf16[4,4,16,384]{3,2,1,0:T(8,128)(2,1)S(1)} %shard_map.82) | data formatting | bytes 393216 | tf_op jit(solution)/shard_map/reshape | solution.py:336
